TPU v7x, 256 devices: a whole 4x4x8 slice. The times are simulated.
256 devices in a mesh: frames: 32 (over y, z), heads: 8 (over x, core).
Axes of the slice: x: 4, y: 4, z: 8, core: 2. Of those that a mesh axis runs over, the one named last changes fastest.
Arguments:
- queries: bfloat16 [36864, 3072], P(('frames', 'heads')), may hold values from -8 to 8
- keys: bfloat16 [36864, 3072], P(('frames', 'heads')), may hold values from -8 to 8
- values: bfloat16 [36864, 3072], P(('frames', 'heads')), may hold values from -6 to 6
- out_grad: bfloat16 [36864, 3072], P(('frames', 'heads')), may hold values from -6 to 6
- windows: int32 [96, 5], replicated, may hold values from -1 to 95, as said below
Outputs:
- query_grad: bfloat16 [36864, 3072], P(('frames', 'heads'))
- key_grad: bfloat16 [36864, 3072], P(('frames', 'heads'))
- value_grad: bfloat16 [36864, 3072], P(('frames', 'heads'))
Inputs may be any that keep to these rules, and one draw needn't show every extreme that they name: Row t of windows starts with t itself; its other 4 entries are distinct tiles other than t whose time row (tile index // 3) differs from that of t by at most one, or -1 for an absent entry.
All inputs are finite; a program needn't handle non-finite values.
Results may differ from a plain program's by a relative error of at most 0.012.
The roundings to bfloat16 on the way count: a program that leaves them out, or rounds other values in their place, can miss the bound.
Values may be sent and summed in bfloat16 or wider, within the bound.
No kernel may reach another device: no remote copies, remote signals or barrier semaphores. Data moves between devices by JAX's collectives and lax.ppermute only.
A program may use at most 256 MiB of HBM per device.

v0:
```python
import jax
import jax.numpy as jnp
from jax import lax
from jax.sharding import PartitionSpec as P

HEAD_DIM = 128
TILE = 384


def with_halo(block, sides, width):
    for axis, dim in sides:
        count = lax.axis_size(axis)
        forward = [(i, i + 1) for i in range(count - 1)]
        backward = [(target, source) for source, target in forward]
        low = lax.ppermute(
            lax.slice_in_dim(block, block.shape[dim] - width, None, axis=dim), axis, forward
        )
        high = lax.ppermute(lax.slice_in_dim(block, 0, width, axis=dim), axis, backward)
        block = jnp.concatenate([low, block, high], axis=dim)
    return block


def masked_scores(query_tile, key_rows, usable, factor):
    scores = (
        jnp.einsum("qhd,wkhd->hqwk", query_tile, key_rows, preferred_element_type=jnp.float32)
        * factor
    )
    return jnp.where(usable[None, None, :, None], scores, -1e30)


def soft_weights(scores, usable, log_sum):
    return jnp.where(usable[None, None, :, None], jnp.exp(scores - log_sum[:, :, None, None]), 0.0)


def front_tile(query_tile, grad_tile, key_rows, value_rows, usable, factor):
    scores = masked_scores(query_tile, key_rows, usable, factor)
    row_max = jnp.max(scores, axis=(2, 3))
    row_sum = jnp.sum(jnp.exp(scores - row_max[:, :, None, None]), axis=(2, 3))
    log_sum = row_max + jnp.log(row_sum)
    weights = soft_weights(scores, usable, log_sum)
    probs = weights.astype(jnp.bfloat16)
    attended = jnp.einsum("hqwk,wkhd->qhd", probs, value_rows, preferred_element_type=jnp.float32)
    row_dot = jnp.sum(grad_tile.astype(jnp.float32) * attended, axis=2).T
    prob_grad = jnp.einsum(
        "qhd,wkhd->hqwk", grad_tile, value_rows, preferred_element_type=jnp.float32
    )
    score_grad = (weights * (prob_grad - row_dot[:, :, None, None])).astype(jnp.bfloat16)
    query_part = (
        jnp.einsum("hqwk,wkhd->qhd", score_grad, key_rows, preferred_element_type=jnp.float32)
        * factor
    )
    return (query_part, probs, score_grad, log_sum, row_dot)


def local(queries, keys, values, out_grad, windows):
    query_loc, key_loc, value_loc, grad_loc = (
        lax.all_to_all(queries, "heads", split_axis=1, concat_axis=0, tiled=True),
        lax.all_to_all(keys, "heads", split_axis=1, concat_axis=0, tiled=True),
        lax.all_to_all(values, "heads", split_axis=1, concat_axis=0, tiled=True),
        lax.all_to_all(out_grad, "heads", split_axis=1, concat_axis=0, tiled=True),
    )
    heads_dev = query_loc.shape[1] // HEAD_DIM
    tile_count = query_loc.shape[0] // TILE
    tile_shape = (tile_count, TILE, heads_dev, HEAD_DIM)
    factor = HEAD_DIM ** (-0.5)
    query_own = query_loc.reshape(tile_shape)
    key_own = key_loc.reshape(tile_shape)
    value_own = value_loc.reshape(tile_shape)
    grad_own = grad_loc.reshape(tile_shape)
    frame_row = lax.axis_index("frames")
    own_lists = lax.dynamic_slice_in_dim(windows, frame_row * tile_count, tile_count, 0)
    pair_pool = with_halo(jnp.stack([key_own, value_own], 1), (("frames", 0),), tile_count)
    key_pool = pair_pool[:, 0]
    value_pool = pair_pool[:, 1]
    usable = own_lists >= 0
    slot_ids = jnp.where(usable, own_lists - (frame_row - 1) * tile_count, 0)

    def front(members):
        query_tile, grad_tile, slot_row, usable_row = members
        return front_tile(
            query_tile, grad_tile, key_pool[slot_row], value_pool[slot_row], usable_row, factor
        )

    query_part, probs, score_grad, log_sum, row_dot = lax.map(
        front, (query_own, grad_own, slot_ids, usable)
    )
    key_part = (
        jnp.einsum("thqwk,tqhd->twkhd", score_grad, query_own, preferred_element_type=jnp.float32)
        * factor
    )
    value_part = jnp.einsum(
        "thqwk,tqhd->twkhd", probs, grad_own, preferred_element_type=jnp.float32
    )
    onehot = (slot_ids[:, :, None] == jnp.arange(3 * tile_count)[None, None, :]).astype(jnp.float32)
    pooled = jnp.einsum(
        "twp,twxkhd->pxkhd",
        onehot,
        jnp.stack([key_part, value_part], 2),
        precision=lax.Precision.HIGHEST,
    )
    outgoing = jnp.concatenate([pooled[:tile_count], pooled[2 * tile_count :]], 0)
    arrived = with_halo(outgoing, (("frames", 0),), tile_count)
    summed = pooled[tile_count : 2 * tile_count] + arrived[:tile_count] + arrived[3 * tile_count :]
    flat_rows = tile_count * TILE
    query_out = query_part.astype(jnp.bfloat16).reshape(flat_rows, -1)
    key_out = summed[:, 0].astype(jnp.bfloat16).reshape(flat_rows, -1)
    value_out = summed[:, 1].astype(jnp.bfloat16).reshape(flat_rows, -1)
    query_back, key_back, value_back = (
        lax.all_to_all(query_out, "heads", split_axis=0, concat_axis=1, tiled=True),
        lax.all_to_all(key_out, "heads", split_axis=0, concat_axis=1, tiled=True),
        lax.all_to_all(value_out, "heads", split_axis=0, concat_axis=1, tiled=True),
    )
    return (query_back, key_back, value_back)


def solution(mesh):
    in_specs = (
        P(("frames", "heads"), None),
        P(("frames", "heads"), None),
        P(("frames", "heads"), None),
        P(("frames", "heads"), None),
        P(),
    )
    out_specs = (
        P(("frames", "heads"), None),
        P(("frames", "heads"), None),
        P(("frames", "heads"), None),
    )
    return jax.shard_map(local, mesh=mesh, in_specs=in_specs, out_specs=out_specs, check_vma=False)
```

profile of v0, /device:TPU:24, one launch (start us, length us, event | category | flops | bytes accessed | tf_op | source)
XLA Modules:
  0.0 478.5 jit_solution(16696609959984328428)
XLA Ops:
  2.8 4.3 all-to-all-start
  9.3 12.0 %all-to-all-done = bf16[144,8,384]{2,0,1:T(8,128)(2,1)S(1)} async-done(((bf16[144,8,384]{2,0,1:T(8,128)(2,1)}), bf16[144,8,384]{2,0,1:T(8,128)(2,1)S(1)}, u32[]{:S(2)}, u32[]{:S(2)}) %all-to-all-start) | async-done | bytes 884768 | tf_op jit(solution)/shard_map/all_to_all | solution.py:58
  21.3 4.2 all-to-all-start.1
  26.3 13.5 %all-to-all-done.1 = bf16[144,8,384]{2,0,1:T(8,128)(2,1)} async-done(((bf16[144,8,384]{2,0,1:T(8,128)(2,1)}), bf16[144,8,384]{2,0,1:T(8,128)(2,1)}, u32[]{:S(2)}, u32[]{:S(2)}) %all-to-all-start.1) | async-done | bytes 884768 | tf_op jit(solution)/shard_map/all_to_all | solution.py:59
  44.5 3.8 collective-permute-start
  48.3 6.0 %collective-permute-start.1 = (bf16[3,2,384,3,128]{4,2,3,1,0:T(8,128)(2,1)}, bf16[3,2,384,3,128]{4,2,3,1,0:T(8,128)(2,1)}, u32[]{:S(2)}, u32[]{:S(2)}) collective-permute-start(bf16[3,2,384,3,128]{4,2,3,1,0:T(8,128)(2,1)} %copy.108), channel_id=1, source_target_pairs={{8,0},{16,8},{24,16},{32,24},{40,32},{48,40},{56,48},{64,56},{72,6... | collective-permute-start | bytes 5308424 | tf_op jit(solution)/shard_map/ppermute | solution.py:18
  55.4 3.6 all-to-all-start.2
  61.1 12.0 %all-to-all-done.2 = bf16[144,8,384]{2,0,1:T(8,128)(2,1)S(1)} async-done(((bf16[144,8,384]{2,0,1:T(8,128)(2,1)}), bf16[144,8,384]{2,0,1:T(8,128)(2,1)S(1)}, u32[]{:S(2)}, u32[]{:S(2)}) %all-to-all-start.2) | async-done | bytes 884768 | tf_op jit(solution)/shard_map/all_to_all | solution.py:57
  73.1 4.2 all-to-all-start.3
  81.3 10.2 %all-to-all-done.3 = bf16[144,8,384]{2,0,1:T(8,128)(2,1)} async-done(((bf16[144,8,384]{2,0,1:T(8,128)(2,1)}), bf16[144,8,384]{2,0,1:T(8,128)(2,1)}, u32[]{:S(2)}, u32[]{:S(2)}) %all-to-all-start.3) | async-done | bytes 884768 | tf_op jit(solution)/shard_map/all_to_all | solution.py:60
  103.3 5.1 %pad_maximum_fusion.1 = bf16[9,2,384,3,128]{4,3,2,0,1:T(4,128)(2,1)S(1)} fusion(bf16[3,2,384,3,128]{4,3,2,0,1:T(4,128)(2,1)S(1)} %copy.111, bf16[3,2,384,3,128]{4,3,2,0,1:T(4,128)(2,1)S(1)} %constant_dynamic-update-slice_fusion, bf16[3,2,384,3,128]{4,3,2,0,1:T(4,128)(2,1)S(1)} %copy.110), kind=kLoop, calls=%fused_computation.35 | loop fusion | flops 5308416 | bytes 10616832 | tf_op jit(solution)/shard_map/concatenate | solution.py:19
  108.4 5.8 %slice_bitcast_fusion = (bf16[9,384,3,128]{3,2,1,0:T(4,128)(2,1)}, bf16[9,384,3,128]{3,2,1,0:T(4,128)(2,1)}) fusion(bf16[9,2,384,3,128]{4,3,2,0,1:T(4,128)(2,1)S(1)} %pad_maximum_fusion.1), kind=kLoop, calls=%fused_computation.37 | loop fusion | bytes 10616832 | tf_op jit(solution)/shard_map/squeeze | solution.py:74
  114.2 143.5 %while.14 = (s32[]{:T(128)}, bf16[3,384,3,128]{1,3,2,0:T(8,128)(2,1)}, bf16[3,3,384,5,384]{2,4,3,1,0:T(8,128)(2,1)}, bf16[3,3,384,5,384]{2,4,3,1,0:T(8,128)(2,1)...) while((s32[]{:T(128)}, ...), condition=%wide.region_4.5_spmd, body=%wide.region_0.4_spmd.sunk | while | flops 2318596864 | bytes 150167472 | solution.py:84
  114.5 5.8 %gather_fusion = bf16[5,384,3,128]{3,2,1,0:T(4,128)(2,1)} fusion(bf16[9,384,3,128]{3,2,1,0:T(4,128)(2,1)} %get-tuple-element.227, s32[1024]{0:T(1024)S(1)} %pad_clamp_fusion.2), kind=kCustom, calls=%fused_computation.clone.1 | custom fusion | bytes 2949140 | tf_op jit(solution)/shard_map/while/body/eval_jaxpr/gather | solution.py:81
  120.3 3.8 copy.176
  129.1 4.2 bitcast_dynamic-update-slice_fusion.5
  133.4 5.8 %gather_fusion.1 = bf16[5,384,3,128]{3,2,1,0:T(4,128)(2,1)} fusion(bf16[9,384,3,128]{3,2,1,0:T(4,128)(2,1)} %get-tuple-element.231, s32[1024]{0:T(1024)S(1)} %pad_clamp_fusion.2), kind=kCustom, calls=%fused_computation.1.clone.1 | custom fusion | bytes 2949140 | tf_op jit(solution)/shard_map/while/body/eval_jaxpr/gather | solution.py:81
  139.2 3.8 copy.177
  143.0 6.6 %fusion.56 = f32[384,3]{0,1:T(4,128)S(1)} fusion(bf16[5,384,3,128]{1,3,0,2:T(8,128)(2,1)S(1)} %copy.177, bf16[3,384,3,128]{3,1,2,0:T(8,128)(2,1)} %get-tuple-element.230, s32[]{:T(128)} %get-tuple-element.211, f32[3,384,5,384]{1,3,2,0:T(8,128)} %copy-done.2, f32[3,384]{1,0:T(4,128)S(1)} %log_add_fusion.2, ...), kind=kOutput, calls=%fused_computation.16.clone.1 | convolution fusion | flops 577731456 | bytes 10626057 | tf_op jit(solution)/shard_map/while/body/eval_jaxpr/hqwk,wkhd->qhd/dot_general | solution.py:42
  149.7 6.1 %bitcast_dynamic-update-slice_fusion.4 = (bf16[3,3,384,5,384]{2,4,3,1,0:T(8,128)(2,1)}, bf16[3,384,5,384]{1,3,2,0:T(8,128)(2,1)S(1)}) fusion(bf16[3,3,384,5,384]{2,4,3,1,0:T(8,128)(2,1)} %get-tuple-element.214, s32[]{:T(128)} %get-tuple-element.211, f32[3,384]{1,0:T(4,128)S(1)} %bitcast.166, bf16[5,384,3,128]{1,3,0,2:T(8,128)(2,1)S(1)} %copy.177, ...), kind=kOutput, calls=%fused_computation.8.clone.1 | convolution fusion | flops 581713920 | bytes 19474436 | tf_op jit(solution)/shard_map/while/body/eval_jaxpr/qhd,wkhd->hqwk/dot_general | solution.py:44
  157.7 5.8 %gather_fusion = bf16[5,384,3,128]{3,2,1,0:T(4,128)(2,1)} fusion(bf16[9,384,3,128]{3,2,1,0:T(4,128)(2,1)} %get-tuple-element.227, s32[1024]{0:T(1024)S(1)} %pad_clamp_fusion.2), kind=kCustom, calls=%fused_computation.clone.1 | custom fusion | bytes 2949140 | tf_op jit(solution)/shard_map/while/body/eval_jaxpr/gather | solution.py:81
  163.6 3.8 copy.176
  172.4 4.3 bitcast_dynamic-update-slice_fusion.5
  176.6 5.8 %gather_fusion.1 = bf16[5,384,3,128]{3,2,1,0:T(4,128)(2,1)} fusion(bf16[9,384,3,128]{3,2,1,0:T(4,128)(2,1)} %get-tuple-element.231, s32[1024]{0:T(1024)S(1)} %pad_clamp_fusion.2), kind=kCustom, calls=%fused_computation.1.clone.1 | custom fusion | bytes 2949140 | tf_op jit(solution)/shard_map/while/body/eval_jaxpr/gather | solution.py:81
  182.5 3.8 copy.177
  186.3 6.6 %fusion.56 = f32[384,3]{0,1:T(4,128)S(1)} fusion(bf16[5,384,3,128]{1,3,0,2:T(8,128)(2,1)S(1)} %copy.177, bf16[3,384,3,128]{3,1,2,0:T(8,128)(2,1)} %get-tuple-element.230, s32[]{:T(128)} %get-tuple-element.211, f32[3,384,5,384]{1,3,2,0:T(8,128)} %copy-done.2, f32[3,384]{1,0:T(4,128)S(1)} %log_add_fusion.2, ...), kind=kOutput, calls=%fused_computation.16.clone.1 | convolution fusion | flops 577731456 | bytes 10626057 | tf_op jit(solution)/shard_map/while/body/eval_jaxpr/hqwk,wkhd->qhd/dot_general | solution.py:42
  193.0 6.2 %bitcast_dynamic-update-slice_fusion.4 = (bf16[3,3,384,5,384]{2,4,3,1,0:T(8,128)(2,1)}, bf16[3,384,5,384]{1,3,2,0:T(8,128)(2,1)S(1)}) fusion(bf16[3,3,384,5,384]{2,4,3,1,0:T(8,128)(2,1)} %get-tuple-element.214, s32[]{:T(128)} %get-tuple-element.211, f32[3,384]{1,0:T(4,128)S(1)} %bitcast.166, bf16[5,384,3,128]{1,3,0,2:T(8,128)(2,1)S(1)} %copy.177, ...), kind=kOutput, calls=%fused_computation.8.clone.1 | convolution fusion | flops 581713920 | bytes 19474436 | tf_op jit(solution)/shard_map/while/body/eval_jaxpr/qhd,wkhd->hqwk/dot_general | solution.py:44
  201.1 5.8 %gather_fusion = bf16[5,384,3,128]{3,2,1,0:T(4,128)(2,1)} fusion(bf16[9,384,3,128]{3,2,1,0:T(4,128)(2,1)} %get-tuple-element.227, s32[1024]{0:T(1024)S(1)} %pad_clamp_fusion.2), kind=kCustom, calls=%fused_computation.clone.1 | custom fusion | bytes 2949140 | tf_op jit(solution)/shard_map/while/body/eval_jaxpr/gather | solution.py:81
  206.9 3.8 copy.176
  215.7 4.3 bitcast_dynamic-update-slice_fusion.5
  220.1 5.8 %gather_fusion.1 = bf16[5,384,3,128]{3,2,1,0:T(4,128)(2,1)} fusion(bf16[9,384,3,128]{3,2,1,0:T(4,128)(2,1)} %get-tuple-element.231, s32[1024]{0:T(1024)S(1)} %pad_clamp_fusion.2), kind=kCustom, calls=%fused_computation.1.clone.1 | custom fusion | bytes 2949140 | tf_op jit(solution)/shard_map/while/body/eval_jaxpr/gather | solution.py:81
  225.9 3.8 copy.177
  229.7 6.6 %fusion.56 = f32[384,3]{0,1:T(4,128)S(1)} fusion(bf16[5,384,3,128]{1,3,0,2:T(8,128)(2,1)S(1)} %copy.177, bf16[3,384,3,128]{3,1,2,0:T(8,128)(2,1)} %get-tuple-element.230, s32[]{:T(128)} %get-tuple-element.211, f32[3,384,5,384]{1,3,2,0:T(8,128)} %copy-done.2, f32[3,384]{1,0:T(4,128)S(1)} %log_add_fusion.2, ...), kind=kOutput, calls=%fused_computation.16.clone.1 | convolution fusion | flops 577731456 | bytes 10626057 | tf_op jit(solution)/shard_map/while/body/eval_jaxpr/hqwk,wkhd->qhd/dot_general | solution.py:42
  236.4 6.1 %bitcast_dynamic-update-slice_fusion.4 = (bf16[3,3,384,5,384]{2,4,3,1,0:T(8,128)(2,1)}, bf16[3,384,5,384]{1,3,2,0:T(8,128)(2,1)S(1)}) fusion(bf16[3,3,384,5,384]{2,4,3,1,0:T(8,128)(2,1)} %get-tuple-element.214, s32[]{:T(128)} %get-tuple-element.211, f32[3,384]{1,0:T(4,128)S(1)} %bitcast.166, bf16[5,384,3,128]{1,3,0,2:T(8,128)(2,1)S(1)} %copy.177, ...), kind=kOutput, calls=%fused_computation.8.clone.1 | convolution fusion | flops 581713920 | bytes 19474436 | tf_op jit(solution)/shard_map/while/body/eval_jaxpr/qhd,wkhd->hqwk/dot_general | solution.py:44
  257.8 7.2 %convolution_bitcast_fusion.2 = f32[3,5,1,384,3,128]{5,3,1,4,0,2:T(8,128)S(1)} fusion(bf16[3,3,384,5,384]{2,4,3,1,0:T(8,128)(2,1)} %get-tuple-element.59, bf16[3,384,3,128,1]{3,2,1,0,4:T(4,128)(2,1)} %bitcast.154), kind=kOutput, calls=%fused_computation.42 | convolution fusion | flops 1698693120 | bytes 23003136 | tf_op jit(solution)/shard_map/thqwk,tqhd->twkhd/dot_general | solution.py:91
  265.0 11.8 %multiply_bitcast_fusion = f32[3,5,1,384,3,128]{5,3,1,4,0,2:T(8,128)} fusion(bf16[3,3,384,5,384]{2,4,3,1,0:T(8,128)(2,1)} %get-tuple-element.58, bf16[3,384,3,128,1]{3,2,1,0,4:T(4,128)(2,1)S(1)} %bitcast.153), kind=kOutput, calls=%fused_computation.34 | convolution fusion | flops 1700904960 | bytes 23003136 | tf_op jit(solution)/shard_map/thqwk,tqhd->twkhd/dot_general | solution.py:88
  276.8 5.8 %pad_maximum_fusion = f32[3,5,2,384,3,128]{5,3,1,4,0,2:T(8,128)S(1)} fusion(f32[3,5,1,384,3,128]{5,3,1,4,0,2:T(8,128)S(1)} %convolution_bitcast_fusion.2, f32[3,5,1,384,3,128]{5,3,1,4,0,2:T(8,128)} %multiply_bitcast_fusion), kind=kLoop, calls=%fused_computation.33 | loop fusion | flops 4423680 | bytes 35389440 | tf_op jit(solution)/shard_map/stack | solution.py:98
  282.6 46.9 %fusion.19 = f32[9,2,384,3,128]{4,0,3,2,1:T(8,128)} fusion(f32[3,5,2,384,3,128]{5,3,1,4,0,2:T(8,128)S(1)} %pad_maximum_fusion, s32[3,5]{1,0:T(4,128)S(1)} %get-tuple-element.239), kind=kOutput, calls=%fused_computation.36 | convolution fusion | flops 477757568 | bytes 28311612 | tf_op jit(solution)/shard_map/twp,twxkhd->pxkhd/dot_general | solution.py:95
  329.4 15.3 %fusion.29 = (f32[3,2,384,3,128]{4,0,3,2,1:T(4,128)}, f32[3,2,384,3,128]{4,0,3,2,1:T(4,128)S(1)}, f32[3,2,384,3,128]{4,0,3,2,1:T(4,128)S(1)}) fusion(f32[9,2,384,3,128]{4,0,3,2,1:T(8,128)} %fusion.19), kind=kLoop, calls=%fused_computation.57 | loop fusion | bytes 21233664 | tf_op jit(solution)/shard_map/slice | solution.py:103
  351.3 6.0 %collective-permute-start.3 = (f32[3,2,384,3,128]{4,2,3,1,0:T(8,128)}, f32[3,2,384,3,128]{4,2,3,1,0:T(8,128)}, u32[]{:S(2)}, u32[]{:S(2)}) collective-permute-start(f32[3,2,384,3,128]{4,2,3,1,0:T(8,128)} %copy.123), channel_id=1, source_target_pairs={{8,0},{16,8},{24,16},{32,24},{40,32},{48,40},{56,48},{64,56},{72,6... | collective-permute-start | bytes 10616840 | tf_op jit(solution)/shard_map/ppermute | solution.py:18
  360.1 3.6 all-to-all-start.4
  363.7 65.7 %collective-permute-done.2 = f32[3,2,384,3,128]{4,2,3,1,0:T(8,128)} collective-permute-done((f32[3,2,384,3,128]{4,2,3,1,0:T(8,128)}, f32[3,2,384,3,128]{4,2,3,1,0:T(8,128)}, u32[]{:S(2)}, u32[]{:S(2)}) %collective-permute-start.2) | collective-permute-done | bytes 3538976 | tf_op jit(solution)/shard_map/ppermute | solution.py:15
  429.4 3.5 collective-permute-done.3
  432.9 5.1 %fusion.23 = bf16[3,2,384,3,128]{4,2,3,1,0:T(8,128)(2,1)S(1)} fusion(f32[3,2,384,3,128]{4,2,3,1,0:T(8,128)} %collective-permute-done.3, f32[3,2,384,3,128]{4,2,3,1,0:T(8,128)} %collective-permute-done.2, f32[3,2,384,3,128]{4,0,3,2,1:T(4,128)} %get-tuple-element.124), kind=kLoop, calls=%fused_computation.41 | loop fusion | flops 2654208 | bytes 12386304 | tf_op jit(solution)/shard_map/convert.1
  440.9 4.2 all-to-all-start.5
  447.9 11.5 %all-to-all-done.5 = bf16[8,144,384]{2,1,0:T(8,128)(2,1)} async-done(((bf16[8,144,384]{2,1,0:T(8,128)(2,1)}), bf16[8,144,384]{2,1,0:T(8,128)(2,1)}, u32[]{:S(2)}, u32[]{:S(2)}) %all-to-all-start.5) | async-done | bytes 884768 | tf_op jit(solution)/shard_map/all_to_all | solution.py:110
  459.4 3.6 all-to-all-start.6
  466.2 10.9 %all-to-all-done.6 = bf16[8,144,384]{2,1,0:T(8,128)(2,1)S(1)} async-done(((bf16[8,144,384]{2,1,0:T(8,128)(2,1)}), bf16[8,144,384]{2,1,0:T(8,128)(2,1)S(1)}, u32[]{:S(2)}, u32[]{:S(2)}) %all-to-all-start.6) | async-done | bytes 884768 | tf_op jit(solution)/shard_map/all_to_all | solution.py:111
  (112 shorter events, 68.9 us)
Async XLA Ops:
  0.6 76.7 %copy-start = (s32[96,5]{0,1:T(8,128)S(1)}, s32[96,5]{0,1:T(8,128)}, u32[]{:S(2)}) copy-start(s32[96,5]{0,1:T(8,128)} %param.11) | copy-start | bytes 5764
  2.8 18.5 %all-to-all-start = ((bf16[144,8,384]{2,0,1:T(8,128)(2,1)}), bf16[144,8,384]{2,0,1:T(8,128)(2,1)S(1)}, u32[]{:S(2)}, u32[]{:S(2)}) async-start(bf16[144,8,384]{2,0,1:T(8,128)(2,1)} %bitcast.116), calls=%async_computation | async-start | bytes 1769472 | tf_op jit(solution)/shard_map/all_to_all | solution.py:58
  21.3 18.4 %all-to-all-start.1 = ((bf16[144,8,384]{2,0,1:T(8,128)(2,1)}), bf16[144,8,384]{2,0,1:T(8,128)(2,1)}, u32[]{:S(2)}, u32[]{:S(2)}) async-start(bf16[144,8,384]{2,0,1:T(8,128)(2,1)} %bitcast.115), calls=%async_computation.1 | async-start | bytes 1769472 | tf_op jit(solution)/shard_map/all_to_all | solution.py:59
  42.3 12.0 %copy-start.6 = (bf16[144,3072]{1,0:T(8,128)(2,1)S(1)}, bf16[144,3072]{1,0:T(8,128)(2,1)}, u32[]{:S(2)}) copy-start(bf16[144,3072]{1,0:T(8,128)(2,1)} %param.7) | copy-start | bytes 2654212
  44.5 52.7 %collective-permute-start = (bf16[3,2,384,3,128]{4,2,3,1,0:T(8,128)(2,1)}, bf16[3,2,384,3,128]{4,2,3,1,0:T(8,128)(2,1)}, u32[]{:S(2)}, u32[]{:S(2)}) collective-permute-start(bf16[3,2,384,3,128]{4,2,3,1,0:T(8,128)(2,1)} %copy.108), channel_id=1, source_target_pairs={{0,8},{8,16},{16,24},{24,32},{32,40},{40,48},{48,56},{56,64},{64,7... | collective-permute-start | bytes 5308424 | tf_op jit(solution)/shard_map/ppermute | solution.py:15
  48.3 51.9 %collective-permute-start.1 = (bf16[3,2,384,3,128]{4,2,3,1,0:T(8,128)(2,1)}, bf16[3,2,384,3,128]{4,2,3,1,0:T(8,128)(2,1)}, u32[]{:S(2)}, u32[]{:S(2)}) collective-permute-start(bf16[3,2,384,3,128]{4,2,3,1,0:T(8,128)(2,1)} %copy.108), channel_id=1, source_target_pairs={{8,0},{16,8},{24,16},{32,24},{40,32},{48,40},{56,48},{64,56},{72,6... | collective-permute-start | bytes 5308424 | tf_op jit(solution)/shard_map/ppermute | solution.py:18
  55.4 17.7 %all-to-all-start.2 = ((bf16[144,8,384]{2,0,1:T(8,128)(2,1)}), bf16[144,8,384]{2,0,1:T(8,128)(2,1)S(1)}, u32[]{:S(2)}, u32[]{:S(2)}) async-start(bf16[144,8,384]{2,0,1:T(8,128)(2,1)} %bitcast.114), calls=%async_computation.2 | async-start | bytes 1769472 | tf_op jit(solution)/shard_map/all_to_all | solution.py:57
  73.1 4.5 copy-start.5
  73.1 18.5 %all-to-all-start.3 = ((bf16[144,8,384]{2,0,1:T(8,128)(2,1)}), bf16[144,8,384]{2,0,1:T(8,128)(2,1)}, u32[]{:S(2)}, u32[]{:S(2)}) async-start(bf16[144,8,384]{2,0,1:T(8,128)(2,1)} %bitcast.113), calls=%async_computation.3 | async-start | bytes 1769472 | tf_op jit(solution)/shard_map/all_to_all | solution.py:60
  80.1 23.1 %copy-start.3 = (bf16[3,384,3,128]{3,2,1,0:T(4,128)(2,1)}, bf16[3,384,3,128]{3,2,1,0:T(4,128)(2,1)S(1)}, u32[]{:S(2)}) copy-start(bf16[3,384,3,128]{3,2,1,0:T(4,128)(2,1)S(1)} %reshape.86) | copy-start | bytes 2654212
  127.3 6.1 %copy-start.2 = (f32[3,384,5,384]{1,3,2,0:T(8,128)}, f32[3,384,5,384]{1,3,2,0:T(8,128)S(1)}, u32[]{:S(2)}) copy-start(f32[3,384,5,384]{1,3,2,0:T(8,128)S(1)} %get-tuple-element.196) | copy-start | bytes 26542084 | tf_op jit(solution)/shard_map/while
  139.2 10.4 %slice-start = ((s8[8847360]{0:T(1024)(128)(4,1)}), s8[458752]{0:T(1024)(128)(4,1)S(1)}, s32[]{:S(2)}) async-start(s8[8847360]{0:T(1024)(128)(4,1)} %bitcast.151), calls=%async_computation.7 | async-start | bytes 917504 | tf_op jit(solution)/shard_map/while
  143.0 6.6 %slice-start.1 = ((s8[8847360]{0:T(1024)(128)(4,1)}), s8[4194304]{0:T(1024)(128)(4,1)S(1)}, s32[]{:S(2)}) async-start(s8[8847360]{0:T(1024)(128)(4,1)} %bitcast.151), calls=%async_computation.8 | async-start | bytes 8388608 | tf_op jit(solution)/shard_map/while
  143.0 6.6 %slice-start.2 = ((s8[8847360]{0:T(1024)(128)(4,1)}), s8[4194304]{0:T(1024)(128)(4,1)S(1)}, s32[]{:S(2)}) async-start(s8[8847360]{0:T(1024)(128)(4,1)} %bitcast.151), calls=%async_computation.9 | async-start | bytes 8388608 | tf_op jit(solution)/shard_map/while
  149.7 6.1 %copy-start.7 = (bf16[3,384,3,128]{1,3,2,0:T(8,128)(2,1)S(1)}, bf16[3,384,3,128]{1,3,2,0:T(8,128)(2,1)}, u32[]{:S(2)}) copy-start(bf16[3,384,3,128]{1,3,2,0:T(8,128)(2,1)} %get-tuple-element.212) | copy-start | bytes 2654212 | tf_op jit(solution)/shard_map/while
  156.8 0.9 copy-start.8
  170.6 6.1 %copy-start.2 = (f32[3,384,5,384]{1,3,2,0:T(8,128)}, f32[3,384,5,384]{1,3,2,0:T(8,128)S(1)}, u32[]{:S(2)}) copy-start(f32[3,384,5,384]{1,3,2,0:T(8,128)S(1)} %get-tuple-element.196) | copy-start | bytes 26542084 | tf_op jit(solution)/shard_map/while
  182.5 10.4 %slice-start = ((s8[8847360]{0:T(1024)(128)(4,1)}), s8[458752]{0:T(1024)(128)(4,1)S(1)}, s32[]{:S(2)}) async-start(s8[8847360]{0:T(1024)(128)(4,1)} %bitcast.151), calls=%async_computation.7 | async-start | bytes 917504 | tf_op jit(solution)/shard_map/while
  186.3 6.6 %slice-start.1 = ((s8[8847360]{0:T(1024)(128)(4,1)}), s8[4194304]{0:T(1024)(128)(4,1)S(1)}, s32[]{:S(2)}) async-start(s8[8847360]{0:T(1024)(128)(4,1)} %bitcast.151), calls=%async_computation.8 | async-start | bytes 8388608 | tf_op jit(solution)/shard_map/while
  186.3 6.6 %slice-start.2 = ((s8[8847360]{0:T(1024)(128)(4,1)}), s8[4194304]{0:T(1024)(128)(4,1)S(1)}, s32[]{:S(2)}) async-start(s8[8847360]{0:T(1024)(128)(4,1)} %bitcast.151), calls=%async_computation.9 | async-start | bytes 8388608 | tf_op jit(solution)/shard_map/while
  192.9 6.2 %copy-start.7 = (bf16[3,384,3,128]{1,3,2,0:T(8,128)(2,1)S(1)}, bf16[3,384,3,128]{1,3,2,0:T(8,128)(2,1)}, u32[]{:S(2)}) copy-start(bf16[3,384,3,128]{1,3,2,0:T(8,128)(2,1)} %get-tuple-element.212) | copy-start | bytes 2654212 | tf_op jit(solution)/shard_map/while
  200.1 0.9 copy-start.8
  213.9 6.2 %copy-start.2 = (f32[3,384,5,384]{1,3,2,0:T(8,128)}, f32[3,384,5,384]{1,3,2,0:T(8,128)S(1)}, u32[]{:S(2)}) copy-start(f32[3,384,5,384]{1,3,2,0:T(8,128)S(1)} %get-tuple-element.196) | copy-start | bytes 26542084 | tf_op jit(solution)/shard_map/while
  225.9 10.4 %slice-start = ((s8[8847360]{0:T(1024)(128)(4,1)}), s8[458752]{0:T(1024)(128)(4,1)S(1)}, s32[]{:S(2)}) async-start(s8[8847360]{0:T(1024)(128)(4,1)} %bitcast.151), calls=%async_computation.7 | async-start | bytes 917504 | tf_op jit(solution)/shard_map/while
  229.7 6.6 %slice-start.1 = ((s8[8847360]{0:T(1024)(128)(4,1)}), s8[4194304]{0:T(1024)(128)(4,1)S(1)}, s32[]{:S(2)}) async-start(s8[8847360]{0:T(1024)(128)(4,1)} %bitcast.151), calls=%async_computation.8 | async-start | bytes 8388608 | tf_op jit(solution)/shard_map/while
  229.7 6.6 %slice-start.2 = ((s8[8847360]{0:T(1024)(128)(4,1)}), s8[4194304]{0:T(1024)(128)(4,1)S(1)}, s32[]{:S(2)}) async-start(s8[8847360]{0:T(1024)(128)(4,1)} %bitcast.151), calls=%async_computation.9 | async-start | bytes 8388608 | tf_op jit(solution)/shard_map/while
  236.4 6.1 %copy-start.7 = (bf16[3,384,3,128]{1,3,2,0:T(8,128)(2,1)S(1)}, bf16[3,384,3,128]{1,3,2,0:T(8,128)(2,1)}, u32[]{:S(2)}) copy-start(bf16[3,384,3,128]{1,3,2,0:T(8,128)(2,1)} %get-tuple-element.212) | copy-start | bytes 2654212 | tf_op jit(solution)/shard_map/while
  243.5 0.9 copy-start.8
  257.8 7.2 %copy-start.4 = (bf16[3,384,3,128]{3,2,1,0:T(4,128)(2,1)S(1)}, bf16[3,384,3,128]{3,2,1,0:T(4,128)(2,1)}, u32[]{:S(2)}) copy-start(bf16[3,384,3,128]{3,2,1,0:T(4,128)(2,1)} %copy-done.3) | copy-start | bytes 2654212
  344.7 12.6 %copy-start.9 = (bf16[3,384,3,128]{1,3,2,0:T(8,128)(2,1)S(1)}, bf16[3,384,3,128]{1,3,2,0:T(8,128)(2,1)}, u32[]{:S(2)}) copy-start(bf16[3,384,3,128]{1,3,2,0:T(8,128)(2,1)} %get-tuple-element.57) | copy-start | bytes 2654212
  347.0 82.4 %collective-permute-start.2 = (f32[3,2,384,3,128]{4,2,3,1,0:T(8,128)}, f32[3,2,384,3,128]{4,2,3,1,0:T(8,128)}, u32[]{:S(2)}, u32[]{:S(2)}) collective-permute-start(f32[3,2,384,3,128]{4,2,3,1,0:T(8,128)} %copy.122), channel_id=1, source_target_pairs={{0,8},{8,16},{16,24},{24,32},{32,40},{40,48},{48,56},{56,64},{64,7... | collective-permute-start | bytes 10616840 | tf_op jit(solution)/shard_map/ppermute | solution.py:15
  351.3 81.6 %collective-permute-start.3 = (f32[3,2,384,3,128]{4,2,3,1,0:T(8,128)}, f32[3,2,384,3,128]{4,2,3,1,0:T(8,128)}, u32[]{:S(2)}, u32[]{:S(2)}) collective-permute-start(f32[3,2,384,3,128]{4,2,3,1,0:T(8,128)} %copy.123), channel_id=1, source_target_pairs={{8,0},{16,8},{24,16},{32,24},{40,32},{48,40},{56,48},{64,56},{72,6... | collective-permute-start | bytes 10616840 | tf_op jit(solution)/shard_map/ppermute | solution.py:18
  360.1 80.8 %all-to-all-start.4 = ((bf16[8,144,384]{2,1,0:T(8,128)(2,1)}), bf16[8,144,384]{2,1,0:T(8,128)(2,1)S(1)}, u32[]{:S(2)}, u32[]{:S(2)}) async-start(bf16[8,144,384]{2,1,0:T(8,128)(2,1)} %all_to_all.98), calls=%async_computation.4 | async-start | bytes 1769472 | tf_op jit(solution)/shard_map/all_to_all | solution.py:109
  438.2 39.9 %copy-start.1 = (s32[96,5]{0,1:T(8,128)S(1)}, s32[96,5]{0,1:T(8,128)}, u32[]{:S(2)}) copy-start(s32[96,5]{0,1:T(8,128)} %param.11) | copy-start | bytes 5764
  440.9 18.4 %all-to-all-start.5 = ((bf16[8,144,384]{2,1,0:T(8,128)(2,1)}), bf16[8,144,384]{2,1,0:T(8,128)(2,1)}, u32[]{:S(2)}, u32[]{:S(2)}) async-start(bf16[8,144,384]{2,1,0:T(8,128)(2,1)} %convert_element_type.26), calls=%async_computation.5 | async-start | bytes 1769472 | tf_op jit(solution)/shard_map/all_to_all | solution.py:110
  459.4 17.7 %all-to-all-start.6 = ((bf16[8,144,384]{2,1,0:T(8,128)(2,1)}), bf16[8,144,384]{2,1,0:T(8,128)(2,1)S(1)}, u32[]{:S(2)}, u32[]{:S(2)}) async-start(bf16[8,144,384]{2,1,0:T(8,128)(2,1)} %convert_element_type.27), calls=%async_computation.6 | async-start | bytes 1769472 | tf_op jit(solution)/shard_map/all_to_all | solution.py:111
where the time goes:
time: 488 us; the launch traced here: 478 us
  waiting for transfers between devices  139 us (28%)
  local copies, waits for them, and re-layouts  128 us (26%)
  matrix products  117 us (24%)
  starting transfers between devices  45.4 us (9%)
  other arithmetic  34.4 us (7%)
  loops' own time  13.9 us (3%)
    ppermute x2, waiting for transfers between devices, with_halo(): lax.ppermute(lax.slice_in_dim(block, block.shape[dim] - width, None, axis...  65.7 us
    dot_general x1, matrix products, local(): jnp.einsum('twp,twxkhd->pxkhd', onehot, jnp.stack([key_part, value_part],...  46.9 us
    gather x6, local copies, waits for them, and re-layouts, front(): value_pool[slot_row]  29 us
    gather x6, local copies, waits for them, and re-layouts, front(): key_pool[slot_row]  28.7 us
    dot_general x3, matrix products, front_tile(): jnp.einsum('hqwk,wkhd->qhd', probs, value_rows, preferred_element_type=jn...  19.7 us
    dot_general x3, matrix products, front_tile(): jnp.einsum('qhd,wkhd->hqwk', grad_tile, value_rows, preferred_element_typ...  18.4 us
    slice x1, local copies, waits for them, and re-layouts, local(): pooled[tile_count:2 * tile_count] + arrived[:tile_count]  15.3 us
    another operation x1, loops' own time, local(): lax.map(front, (query_own, grad_own, slot_ids, usable))  13.9 us
  transfers between devices with their start and end apart: 11, of which 8 were waited for; matrix products, arithmetic and copies ran while one was open for 7% of the time, Pallas kernels for 0%

commit v1 on v0

v1 whole, which is shorter than its diff:
```python
import functools

import jax
import jax.numpy as jnp
from jax import lax
from jax.experimental import pallas as pl
from jax.experimental.pallas import tpu as pltpu
from jax.sharding import PartitionSpec as P

HEAD_DIM = 128
TILE = 384
WIN = 5
PAIR = 2 * HEAD_DIM
SUB = 128
SUBS = TILE // SUB
NEG = -1e30
LOG2E = 1.4426950408889634
NT = (((1,), (1,)), ((), ()))
TN = (((0,), (0,)), ((), ()))


def pack_kernel(groups, a_ref, b_ref, out_ref):
    for g in range(groups):
        cols = slice(g * HEAD_DIM, (g + 1) * HEAD_DIM)
        out_ref[g, :, :HEAD_DIM] = a_ref[:, cols]
        out_ref[g, :, HEAD_DIM:] = b_ref[:, cols]


def pack(a, b, chunk, groups):
    rows = a.shape[0]
    block = pl.BlockSpec((rows, groups * HEAD_DIM), lambda i: (0, chunk))
    return pl.pallas_call(
        functools.partial(pack_kernel, groups),
        grid=(1,),
        out_shape=jax.ShapeDtypeStruct((groups, rows, PAIR), a.dtype),
        in_specs=[block, block],
        out_specs=pl.BlockSpec((groups, rows, PAIR), lambda i: (0, 0, 0)),
        cost_estimate=pl.CostEstimate(
            flops=0, bytes_accessed=groups * rows * PAIR * 4, transcendentals=0
        ),
        name="pack",
    )(a, b)


def unpack_kernel(groups, dq_ref, dkv_ref, *refs):
    out_q, out_k, out_v = refs[-3:]
    for g in range(groups):
        cols = slice(g * HEAD_DIM, (g + 1) * HEAD_DIM)
        out_q[:, cols] = dq_ref[g]
        out_k[:, cols] = dkv_ref[g, :, :HEAD_DIM]
        out_v[:, cols] = dkv_ref[g, :, HEAD_DIM:]


def unpack(dq, dkv, before, chunk, chunks):
    groups, rows, _ = dq.shape
    out_block = pl.BlockSpec((rows, groups * HEAD_DIM), lambda i: (0, chunk))
    shape = jax.ShapeDtypeStruct((rows, chunks * groups * HEAD_DIM), dq.dtype)
    return pl.pallas_call(
        functools.partial(unpack_kernel, groups),
        grid=(1,),
        out_shape=[shape] * 3,
        in_specs=[
            pl.BlockSpec(dq.shape, lambda i: (0, 0, 0)),
            pl.BlockSpec(dkv.shape, lambda i: (0, 0, 0)),
        ]
        + [pl.BlockSpec(memory_space=pl.ANY)] * len(before),
        out_specs=[out_block] * 3,
        input_output_aliases={2 + i: i for i in range(len(before))},
        cost_estimate=pl.CostEstimate(
            flops=0, bytes_accessed=groups * rows * HEAD_DIM * 12, transcendentals=0
        ),
        name="unpack",
    )(dq, dkv, *before)


def attend_kernel(
    tiles,
    slot_ref,
    qg_hbm,
    own_hbm,
    prev_hbm,
    next_hbm,
    dq_ref,
    dprev_ref,
    down_ref,
    dnext_ref,
    qg_ref,
    kv_ref,
    acc_ref,
    both_ref,
    score_ref,
    pgrad_ref,
    grad_ref,
    sems,
):
    rows = tiles * TILE
    copies = [
        pltpu.make_async_copy(qg_hbm, qg_ref, sems.at[0]),
        pltpu.make_async_copy(own_hbm, kv_ref.at[pl.ds(rows, rows)], sems.at[1]),
        pltpu.make_async_copy(prev_hbm, kv_ref.at[pl.ds(0, rows)], sems.at[2]),
        pltpu.make_async_copy(next_hbm, kv_ref.at[pl.ds(2 * rows, rows)], sems.at[3]),
    ]
    for copy in copies:
        copy.start()
    acc_ref[...] = jnp.zeros_like(acc_ref)
    both_ref[...] = jnp.zeros_like(both_ref)
    for copy in copies:
        copy.wait()
    factor = HEAD_DIM ** (-0.5)
    scale = factor * LOG2E

    def one_tile(t, carry):
        base = pl.multiple_of(t * TILE, TILE)
        both_ref[:TILE, :HEAD_DIM] = qg_ref[pl.ds(base, TILE), :HEAD_DIM]
        both_ref[TILE:, HEAD_DIM:] = qg_ref[pl.ds(base, TILE), HEAD_DIM:]
        used = [slot_ref[t, j] >= 0 for j in range(WIN)]
        places = [
            pl.multiple_of(jnp.maximum(slot_ref[t, j], 0) * TILE, TILE) for j in range(WIN)
        ]
        both = both_ref[...]
        top = jnp.full((1, TILE), NEG, jnp.float32)
        for j in range(WIN):
            for s in range(SUBS):
                kv = kv_ref[pl.ds(places[j] + s * SUB, SUB), :]
                out = lax.dot_general(kv, both, NT, preferred_element_type=jnp.float32)
                score = out[:, :TILE]
                score_ref[j, s * SUB : (s + 1) * SUB, :] = score
                pgrad_ref[j, s * SUB : (s + 1) * SUB, :] = out[:, TILE:]
                here = jnp.max(score, axis=0, keepdims=True)
                top = jnp.maximum(top, jnp.where(used[j], here, NEG))
        top = top * scale
        total = jnp.zeros((1, TILE), jnp.float32)
        for j in range(WIN):
            shift = jnp.where(used[j], top, -NEG)
            for s in range(SUBS):
                part = slice(s * SUB, (s + 1) * SUB)
                weight = jnp.exp2(score_ref[j, part, :] * scale - shift)
                score_ref[j, part, :] = weight
                total = total + jnp.sum(weight, axis=0, keepdims=True)
        inverse = 1.0 / total
        row_dot = jnp.zeros((1, TILE), jnp.float32)
        for j in range(WIN):
            for s in range(SUBS):
                part = slice(s * SUB, (s + 1) * SUB)
                prob = (score_ref[j, part, :] * inverse).astype(jnp.bfloat16)
                grad_ref[j, part, TILE:] = prob
                row_dot = row_dot + jnp.sum(
                    prob.astype(jnp.float32) * pgrad_ref[j, part, :], axis=0, keepdims=True
                )
        for j in range(WIN):
            for s in range(SUBS):
                part = slice(s * SUB, (s + 1) * SUB)
                weight = score_ref[j, part, :] * inverse
                grad_ref[j, part, :TILE] = (weight * (pgrad_ref[j, part, :] - row_dot)).astype(
                    jnp.bfloat16
                )
        dq = jnp.zeros((TILE, HEAD_DIM), jnp.float32)
        for j in range(WIN):
            place = pl.ds(places[j], TILE)
            acc_ref[place, :] += jnp.dot(
                grad_ref[j], both, preferred_element_type=jnp.float32
            )
            dq = dq + lax.dot_general(
                grad_ref[j, :, :TILE],
                kv_ref[place, :HEAD_DIM],
                TN,
                preferred_element_type=jnp.float32,
            )
        dq_ref[pl.ds(base, TILE), :] = (dq * factor).astype(dq_ref.dtype)
        return carry

    lax.fori_loop(0, tiles, one_tile, 0)
    lanes = lax.broadcasted_iota(jnp.int32, (1, PAIR), 1)
    side = jnp.where(lanes < HEAD_DIM, jnp.float32(factor), jnp.float32(1.0))
    dprev_ref[...] = (acc_ref[:rows, :] * side).astype(dprev_ref.dtype)
    down_ref[...] = acc_ref[rows : 2 * rows, :] * side
    dnext_ref[...] = (acc_ref[2 * rows :, :] * side).astype(dnext_ref.dtype)


def attend(slots, qg, own, prev, after):
    rows = qg.shape[0]
    tiles = rows // TILE
    hbm = pl.BlockSpec(memory_space=pl.ANY)
    vmem = pl.BlockSpec(memory_space=pltpu.VMEM)
    return pl.pallas_call(
        functools.partial(attend_kernel, tiles),
        out_shape=[
            jax.ShapeDtypeStruct((rows, HEAD_DIM), qg.dtype),
            jax.ShapeDtypeStruct((rows, PAIR), qg.dtype),
            jax.ShapeDtypeStruct((rows, PAIR), jnp.float32),
            jax.ShapeDtypeStruct((rows, PAIR), qg.dtype),
        ],
        in_specs=[pl.BlockSpec(memory_space=pltpu.SMEM), hbm, hbm, hbm, hbm],
        out_specs=[vmem] * 4,
        scratch_shapes=[
            pltpu.VMEM((rows, PAIR), qg.dtype),
            pltpu.VMEM((3 * rows, PAIR), qg.dtype),
            pltpu.VMEM((3 * rows, PAIR), jnp.float32),
            pltpu.VMEM((2 * TILE, PAIR), qg.dtype),
            pltpu.VMEM((WIN, TILE, TILE), jnp.float32),
            pltpu.VMEM((WIN, TILE, TILE), jnp.float32),
            pltpu.VMEM((WIN, TILE, 2 * TILE), qg.dtype),
            pltpu.SemaphoreType.DMA((4,)),
        ],
        compiler_params=pltpu.CompilerParams(vmem_limit_bytes=40 * 1024 * 1024),
        cost_estimate=pl.CostEstimate(
            flops=tiles * WIN * 10 * TILE * TILE * PAIR,
            bytes_accessed=rows * PAIR * 16,
            transcendentals=tiles * WIN * TILE * TILE,
        ),
        name="attend",
    )(slots, qg, own, prev, after)


def regroup(x):
    return lax.all_to_all(x, "heads", split_axis=0, concat_axis=0, tiled=True)


def to_neighbours(to_prev, to_next):
    count = lax.axis_size("frames")
    up = [(i, i + 1) for i in range(count - 1)]
    down = [(target, source) for source, target in up]
    from_prev = lax.ppermute(to_next, "frames", up)
    from_next = lax.ppermute(to_prev, "frames", down)
    return from_prev, from_next


def local(queries, keys, values, out_grad, windows):
    groups = lax.axis_size("heads")
    chunks = queries.shape[1] // (groups * HEAD_DIM)
    rows = queries.shape[0] * groups
    tiles = rows // TILE
    frame = lax.axis_index("frames")
    lists = lax.dynamic_slice_in_dim(windows, frame * tiles, tiles, 0)
    slots = jnp.where(lists >= 0, lists - (frame - 1) * tiles, -1)
    outs = ()
    for c in range(chunks):
        kv = regroup(pack(keys, values, c, groups)).reshape(rows, PAIR)
        qg = regroup(pack(queries, out_grad, c, groups)).reshape(rows, PAIR)
        prev, after = to_neighbours(kv, kv)
        dq, dprev, down, dnext = attend(slots, qg, kv, prev, after)
        from_prev, from_next = to_neighbours(dprev, dnext)
        dkv = (down + from_prev.astype(jnp.float32) + from_next.astype(jnp.float32)).astype(
            queries.dtype
        )
        dq = regroup(dq.reshape(groups, -1, HEAD_DIM))
        dkv = regroup(dkv.reshape(groups, -1, PAIR))
        outs = unpack(dq, dkv, outs, c, chunks)
    return tuple(outs)


def solution(mesh):
    spec = P(("frames", "heads"), None)
    return jax.shard_map(
        local, mesh=mesh, in_specs=(spec,) * 4 + (P(),), out_specs=(spec,) * 3, check_vma=False
    )
```

time: 488 us -> 245 us (0.50); the launches traced: 478 us -> 243 us
  local copies, waits for them, and re-layouts: 128 us -> 7.15 us
  matrix products: 117 us -> 0 us
  waiting for transfers between devices: 139 us -> 56.4 us
  Pallas kernels: 0 us -> 76.8 us
  starting transfers between devices: 45.4 us -> 94.9 us
  other arithmetic: 34.4 us -> 6.91 us
  loops' own time: 13.9 us -> 0 us
    dot_general x15 -> x0, matrix products: 117 us -> none  [the longest x1 46.9 us: local(): jnp.einsum('twp,twxkhd->pxkhd', onehot, jnp.stack([key_part, value_part],...]
    pallas_call x0 -> x12, Pallas kernels: none -> 76.8 us  [the longest x3 58 us: attend(): pl.pallas_call(functools.partial(attend_kernel, tiles), out_shape=[jax.Sh...]
    ppermute x4 -> x12, waiting for transfers between devices: 69.2 us -> 0.03 us  [the longest x6 0.02 us: to_neighbours(): from_prev = lax.ppermute(to_next, 'frames', up)]
    gather x12 -> x0, local copies, waits for them, and re-layouts: 57.7 us -> none  [the longest x6 29 us: front(): value_pool[slot_row]]
    ppermute x4 -> x12, starting transfers between devices: 17.8 us -> 45.5 us  [the longest x6 30.1 us: to_neighbours(): from_next = lax.ppermute(to_prev, 'frames', down)]
    all_to_all x7 -> x12, starting transfers between devices: 27.7 us -> 49.4 us  [regroup(): return lax.all_to_all(x, 'heads', split_axis=0, concat_axis=0, tiled=True)]
    slice x6 -> x0, local copies, waits for them, and re-layouts: 21.6 us -> none  [the longest x1 15.3 us: local(): pooled[tile_count:2 * tile_count] + arrived[:tile_count]]
    another operation x1 -> x0, loops' own time: 13.9 us -> none  [local(): lax.map(front, (query_own, grad_own, slot_ids, usable))]
  transfers between devices with their start and end apart: 11 -> 24, of which waited for: 8 -> 7; matrix products, arithmetic and copies ran while one was open for 7% -> 3% of each run, Pallas kernels for 0% -> 30%
where the time goes in v1:
time: 245 us; the launch traced here: 243 us
  starting transfers between devices  94.9 us (39%)
  Pallas kernels  76.8 us (31%)
  waiting for transfers between devices  56.4 us (23%)
  local copies, waits for them, and re-layouts  7.15 us (3%)
  other arithmetic  6.91 us (3%)
    pallas_call x3, Pallas kernels, attend(): pl.pallas_call(functools.partial(attend_kernel, tiles), out_shape=[jax.Sh...  58 us
    all_to_all x12, waiting for transfers between devices, regroup(): return lax.all_to_all(x, 'heads', split_axis=0, concat_axis=0, tiled=True)  56.4 us
    all_to_all x12, starting transfers between devices, regroup(): return lax.all_to_all(x, 'heads', split_axis=0, concat_axis=0, tiled=True)  49.4 us
    ppermute x6, starting transfers between devices, to_neighbours(): from_next = lax.ppermute(to_prev, 'frames', down)  30.1 us
    ppermute x6, starting transfers between devices, to_neighbours(): from_prev = lax.ppermute(to_next, 'frames', up)  15.4 us
    pallas_call x6, Pallas kernels, pack(): pl.pallas_call(functools.partial(pack_kernel, groups), grid=(1,), out_sha...  11.8 us
    unnamed x27, local copies, waits for them, and re-layouts  7.07 us
    pallas_call x3, Pallas kernels, unpack(): pl.pallas_call(functools.partial(unpack_kernel, groups), grid=(1,), out_s...  6.94 us
  transfers between devices with their start and end apart: 24, of which 7 were waited for; matrix products, arithmetic and copies ran while one was open for 3% of the time, Pallas kernels for 30%

profile of v1, /device:TPU:24, one launch (start us, length us, event | category | flops | bytes accessed | tf_op | source)
XLA Modules:
  0.0 243.2 jit_solution(3801994996438432435)
XLA Ops:
  0.6 2.0 pack.6
  2.6 4.3 %all-to-all-start = ((bf16[8,144,256]{2,1,0:T(8,128)(2,1)}), bf16[8,144,256]{2,1,0:T(8,128)(2,1)S(1)}, u32[]{:S(2)}, u32[]{:S(2)}) async-start(bf16[8,144,256]{2,1,0:T(8,128)(2,1)} %pack.6), calls=%async_computation | async-start | bytes 1179648 | tf_op jit(solution)/shard_map/all_to_all | solution.py:216
  6.9 2.0 pack.7
  8.9 9.1 %all-to-all-done = bf16[8,144,256]{2,1,0:T(8,128)(2,1)S(1)} async-done(((bf16[8,144,256]{2,1,0:T(8,128)(2,1)}), bf16[8,144,256]{2,1,0:T(8,128)(2,1)S(1)}, u32[]{:S(2)}, u32[]{:S(2)}) %all-to-all-start) | async-done | bytes 589856 | tf_op jit(solution)/shard_map/all_to_all | solution.py:216
  18.0 3.5 %all-to-all-start.1 = ((bf16[8,144,256]{2,1,0:T(8,128)(2,1)}), bf16[8,144,256]{2,1,0:T(8,128)(2,1)S(1)}, u32[]{:S(2)}, u32[]{:S(2)}) async-start(bf16[8,144,256]{2,1,0:T(8,128)(2,1)} %pack.7), calls=%async_computation.1 | async-start | bytes 1179648 | tf_op jit(solution)/shard_map/all_to_all | solution.py:216
  21.5 2.0 pack.9
  23.5 9.0 %all-to-all-done.1 = bf16[8,144,256]{2,1,0:T(8,128)(2,1)S(1)} async-done(((bf16[8,144,256]{2,1,0:T(8,128)(2,1)}), bf16[8,144,256]{2,1,0:T(8,128)(2,1)S(1)}, u32[]{:S(2)}, u32[]{:S(2)}) %all-to-all-start.1) | async-done | bytes 589856 | tf_op jit(solution)/shard_map/all_to_all | solution.py:216
  32.5 3.5 %all-to-all-start.5 = ((bf16[8,144,256]{2,1,0:T(8,128)(2,1)}), bf16[8,144,256]{2,1,0:T(8,128)(2,1)S(1)}, u32[]{:S(2)}, u32[]{:S(2)}) async-start(bf16[8,144,256]{2,1,0:T(8,128)(2,1)} %pack.9), calls=%async_computation.5 | async-start | bytes 1179648 | tf_op jit(solution)/shard_map/all_to_all | solution.py:216
  36.0 2.0 pack.11
  38.0 9.0 %all-to-all-done.5 = bf16[8,144,256]{2,1,0:T(8,128)(2,1)S(1)} async-done(((bf16[8,144,256]{2,1,0:T(8,128)(2,1)}), bf16[8,144,256]{2,1,0:T(8,128)(2,1)S(1)}, u32[]{:S(2)}, u32[]{:S(2)}) %all-to-all-start.5) | async-done | bytes 589856 | tf_op jit(solution)/shard_map/all_to_all | solution.py:216
  47.0 3.5 %all-to-all-start.9 = ((bf16[8,144,256]{2,1,0:T(8,128)(2,1)}), bf16[8,144,256]{2,1,0:T(8,128)(2,1)S(1)}, u32[]{:S(2)}, u32[]{:S(2)}) async-start(bf16[8,144,256]{2,1,0:T(8,128)(2,1)} %pack.11), calls=%async_computation.9 | async-start | bytes 1179648 | tf_op jit(solution)/shard_map/all_to_all | solution.py:216
  50.6 3.9 %collective-permute-start = (bf16[1152,256]{1,0:T(8,128)(2,1)S(1)}, bf16[1152,256]{1,0:T(8,128)(2,1)S(1)}, u32[]{:S(2)}, u32[]{:S(2)}) collective-permute-start(bf16[1152,256]{1,0:T(8,128)(2,1)S(1)} %bitcast.19), channel_id=1, source_target_pairs={{0,8},{8,16},{16,24},{24,32},{32,40},{40,48},{48,56},{56,64},{64,7... | collective-permute-start | bytes 1769480 | tf_op jit(solution)/shard_map/ppermute | solution.py:223
  54.4 6.0 %collective-permute-start.1 = (bf16[1152,256]{1,0:T(8,128)(2,1)S(1)}, bf16[1152,256]{1,0:T(8,128)(2,1)}, u32[]{:S(2)}, u32[]{:S(2)}) collective-permute-start(bf16[1152,256]{1,0:T(8,128)(2,1)S(1)} %bitcast.20), channel_id=1, source_target_pairs={{8,0},{16,8},{24,16},{32,24},{40,32},{48,40},{56,48},{64,56},{72,6... | collective-permute-start | bytes 1769480 | tf_op jit(solution)/shard_map/ppermute | solution.py:224
  60.5 2.0 pack.8
  62.4 4.7 %all-to-all-start.4 = ((bf16[8,144,256]{2,1,0:T(8,128)(2,1)}), bf16[8,144,256]{2,1,0:T(8,128)(2,1)S(1)}, u32[]{:S(2)}, u32[]{:S(2)}) async-start(bf16[8,144,256]{2,1,0:T(8,128)(2,1)} %pack.8), calls=%async_computation.4 | async-start | bytes 1179648 | tf_op jit(solution)/shard_map/all_to_all | solution.py:216
  67.3 1.9 collective-permute-start.4
  69.2 6.0 %collective-permute-start.5 = (bf16[1152,256]{1,0:T(8,128)(2,1)S(1)}, bf16[1152,256]{1,0:T(8,128)(2,1)}, u32[]{:S(2)}, u32[]{:S(2)}) collective-permute-start(bf16[1152,256]{1,0:T(8,128)(2,1)S(1)} %bitcast.16), channel_id=1, source_target_pairs={{8,0},{16,8},{24,16},{32,24},{40,32},{48,40},{56,48},{64,56},{72,6... | collective-permute-start | bytes 1769480 | tf_op jit(solution)/shard_map/ppermute | solution.py:224
  75.3 2.0 pack.10
  77.2 1.9 collective-permute-start.8
  79.2 4.8 %all-to-all-start.8 = ((bf16[8,144,256]{2,1,0:T(8,128)(2,1)}), bf16[8,144,256]{2,1,0:T(8,128)(2,1)}, u32[]{:S(2)}, u32[]{:S(2)}) async-start(bf16[8,144,256]{2,1,0:T(8,128)(2,1)} %pack.10), calls=%async_computation.8 | async-start | bytes 1179648 | tf_op jit(solution)/shard_map/all_to_all | solution.py:216
  84.8 6.0 %collective-permute-start.9 = (bf16[1152,256]{1,0:T(8,128)(2,1)S(1)}, bf16[1152,256]{1,0:T(8,128)(2,1)}, u32[]{:S(2)}, u32[]{:S(2)}) collective-permute-start(bf16[1152,256]{1,0:T(8,128)(2,1)S(1)} %bitcast.13), channel_id=1, source_target_pairs={{8,0},{16,8},{24,16},{32,24},{40,32},{48,40},{56,48},{64,56},{72,6... | collective-permute-start | bytes 1769480 | tf_op jit(solution)/shard_map/ppermute | solution.py:224
  90.9 1.1 copy-done.9
  92.0 19.3 %attend.3 = (bf16[1152,128]{1,0:T(8,128)(2,1)S(1)}, bf16[1152,256]{1,0:T(8,128)(2,1)}, f32[1152,256]{1,0:T(8,128)S(1)}, bf16[1152,256]{1,0:T(8,128)(2,1)}) custom-call(s32[3,5]{1,0:T(4,128)S(1)} %subtract_select_fusion.slot_ref, bf16[1152,256]{1,0:T(8,128)(2,1)S(1)} %bitcast.18, bf16[1152,256]{1,0:T(8,128)(2,1)S(1)} %bitcast.21, ...), custom_call_target="tpu_custom_call" | custom-call | flops 5662310400 | bytes 4718592 | tf_op jit(solution)/shard_map/attend/pallas_call | solution.py:185
  112.0 4.8 %all-to-all-start.2 = ((bf16[8,144,128]{2,1,0:T(8,128)(2,1)}), bf16[8,144,128]{2,1,0:T(8,128)(2,1)}, u32[]{:S(2)}, u32[]{:S(2)}) async-start(bf16[8,144,128]{2,1,0:T(8,128)(2,1)} %bitcast.25), calls=%async_computation.2 | async-start | bytes 589824 | tf_op jit(solution)/shard_map/all_to_all | solution.py:216
  116.8 1.1 copy-done.4
  117.8 19.4 %attend.4 = (bf16[1152,128]{1,0:T(8,128)(2,1)S(1)}, bf16[1152,256]{1,0:T(8,128)(2,1)}, f32[1152,256]{1,0:T(8,128)S(1)}, bf16[1152,256]{1,0:T(8,128)(2,1)}) custom-call(s32[3,5]{1,0:T(4,128)S(1)} %subtract_select_fusion.slot_ref, bf16[1152,256]{1,0:T(8,128)(2,1)S(1)} %bitcast.22, bf16[1152,256]{1,0:T(8,128)(2,1)S(1)} %bitcast.17, ...), custom_call_target="tpu_custom_call" | custom-call | flops 5662310400 | bytes 4718592 | tf_op jit(solution)/shard_map/attend/pallas_call | solution.py:185
  137.9 1.9 collective-permute-start.7
  139.8 3.9 %collective-permute-start.6 = (bf16[1152,256]{1,0:T(8,128)(2,1)}, bf16[1152,256]{1,0:T(8,128)(2,1)}, u32[]{:S(2)}, u32[]{:S(2)}) collective-permute-start(bf16[1152,256]{1,0:T(8,128)(2,1)} %get-tuple-element.27), channel_id=1, source_target_pairs={{0,8},{8,16},{16,24},{24,32},{32,40},{40,48},{48,56},{56,64},{64,7... | collective-permute-start | bytes 1769480 | tf_op jit(solution)/shard_map/ppermute | solution.py:223
  143.8 4.8 %all-to-all-start.6 = ((bf16[8,144,128]{2,1,0:T(8,128)(2,1)}), bf16[8,144,128]{2,1,0:T(8,128)(2,1)}, u32[]{:S(2)}, u32[]{:S(2)}) async-start(bf16[8,144,128]{2,1,0:T(8,128)(2,1)} %bitcast.23), calls=%async_computation.6 | async-start | bytes 589824 | tf_op jit(solution)/shard_map/all_to_all | solution.py:216
  149.7 19.3 %attend.5 = (bf16[1152,128]{1,0:T(8,128)(2,1)S(1)}, bf16[1152,256]{1,0:T(8,128)(2,1)}, f32[1152,256]{1,0:T(8,128)S(1)}, bf16[1152,256]{1,0:T(8,128)(2,1)}) custom-call(s32[3,5]{1,0:T(4,128)S(1)} %subtract_select_fusion.slot_ref, bf16[1152,256]{1,0:T(8,128)(2,1)} %bitcast.8.qg_hbm, bf16[1152,256]{1,0:T(8,128)(2,1)S(1)} %bitcast.14, ...), custom_call_target="tpu_custom_call" | custom-call | flops 5662310400 | bytes 4718592 | tf_op jit(solution)/shard_map/attend/pallas_call | solution.py:185
  169.8 4.0 %collective-permute-start.11 = (bf16[1152,256]{1,0:T(8,128)(2,1)}, bf16[1152,256]{1,0:T(8,128)(2,1)}, u32[]{:S(2)}, u32[]{:S(2)}) collective-permute-start(bf16[1152,256]{1,0:T(8,128)(2,1)} %get-tuple-element.32), channel_id=1, source_target_pairs={{8,0},{16,8},{24,16},{32,24},{40,32},{48,40},{56,48},{64,56},{72,6... | collective-permute-start | bytes 1769480 | tf_op jit(solution)/shard_map/ppermute | solution.py:224
  173.8 1.9 collective-permute-start.10
  175.7 6.0 %collective-permute-start.3 = (bf16[1152,256]{1,0:T(8,128)(2,1)}, bf16[1152,256]{1,0:T(8,128)(2,1)}, u32[]{:S(2)}, u32[]{:S(2)}) collective-permute-start(bf16[1152,256]{1,0:T(8,128)(2,1)} %get-tuple-element.24), channel_id=1, source_target_pairs={{8,0},{16,8},{24,16},{32,24},{40,32},{48,40},{56,48},{64,56},{72,6... | collective-permute-start | bytes 1769480 | tf_op jit(solution)/shard_map/ppermute | solution.py:224
  181.8 1.9 collective-permute-start.2
  183.7 4.8 %all-to-all-start.10 = ((bf16[8,144,128]{2,1,0:T(8,128)(2,1)}), bf16[8,144,128]{2,1,0:T(8,128)(2,1)}, u32[]{:S(2)}, u32[]{:S(2)}) async-start(bf16[8,144,128]{2,1,0:T(8,128)(2,1)} %bitcast.24), calls=%async_computation.10 | async-start | bytes 589824 | tf_op jit(solution)/shard_map/all_to_all | solution.py:216
  188.5 2.3 add_convert_fusion.1
  190.8 5.7 %all-to-all-done.10.dq_ref = bf16[8,144,128]{2,1,0:T(8,128)(2,1)} async-done(((bf16[8,144,128]{2,1,0:T(8,128)(2,1)}), bf16[8,144,128]{2,1,0:T(8,128)(2,1)}, u32[]{:S(2)}, u32[]{:S(2)}) %all-to-all-start.10) | async-done | bytes 294944 | tf_op jit(solution)/shard_map/all_to_all | solution.py:216
  196.5 3.5 %all-to-all-start.7 = ((bf16[8,144,256]{2,1,0:T(8,128)(2,1)}), bf16[8,144,256]{2,1,0:T(8,128)(2,1)S(1)}, u32[]{:S(2)}, u32[]{:S(2)}) async-start(bf16[8,144,256]{2,1,0:T(8,128)(2,1)} %bitcast.26), calls=%async_computation.7 | async-start | bytes 1179648 | tf_op jit(solution)/shard_map/all_to_all | solution.py:216
  200.1 2.3 add_convert_fusion
  202.4 8.6 %all-to-all-done.7.dkv_ref = bf16[8,144,256]{2,1,0:T(8,128)(2,1)S(1)} async-done(((bf16[8,144,256]{2,1,0:T(8,128)(2,1)}), bf16[8,144,256]{2,1,0:T(8,128)(2,1)S(1)}, u32[]{:S(2)}, u32[]{:S(2)}) %all-to-all-start.7) | async-done | bytes 589856 | tf_op jit(solution)/shard_map/all_to_all | solution.py:216
  211.0 3.5 %all-to-all-start.11 = ((bf16[8,144,256]{2,1,0:T(8,128)(2,1)}), bf16[8,144,256]{2,1,0:T(8,128)(2,1)S(1)}, u32[]{:S(2)}, u32[]{:S(2)}) async-start(bf16[8,144,256]{2,1,0:T(8,128)(2,1)} %bitcast.11), calls=%async_computation.11 | async-start | bytes 1179648 | tf_op jit(solution)/shard_map/all_to_all | solution.py:216
  214.6 2.3 add_convert_fusion.2
  216.9 8.6 %all-to-all-done.11.dkv_ref = bf16[8,144,256]{2,1,0:T(8,128)(2,1)S(1)} async-done(((bf16[8,144,256]{2,1,0:T(8,128)(2,1)}), bf16[8,144,256]{2,1,0:T(8,128)(2,1)S(1)}, u32[]{:S(2)}, u32[]{:S(2)}) %all-to-all-start.11) | async-done | bytes 589856 | tf_op jit(solution)/shard_map/all_to_all | solution.py:216
  225.6 3.5 %all-to-all-start.3 = ((bf16[8,144,256]{2,1,0:T(8,128)(2,1)}), bf16[8,144,256]{2,1,0:T(8,128)(2,1)S(1)}, u32[]{:S(2)}, u32[]{:S(2)}) async-start(bf16[8,144,256]{2,1,0:T(8,128)(2,1)} %bitcast.3), calls=%async_computation.3 | async-start | bytes 1179648 | tf_op jit(solution)/shard_map/all_to_all | solution.py:216
  229.1 2.3 unpack.3
  231.4 2.3 unpack.4
  233.7 6.3 %all-to-all-done.3.dkv_ref = bf16[8,144,256]{2,1,0:T(8,128)(2,1)S(1)} async-done(((bf16[8,144,256]{2,1,0:T(8,128)(2,1)}), bf16[8,144,256]{2,1,0:T(8,128)(2,1)S(1)}, u32[]{:S(2)}, u32[]{:S(2)}) %all-to-all-start.3) | async-done | bytes 589856 | tf_op jit(solution)/shard_map/all_to_all | solution.py:216
  240.9 2.3 unpack.5
  (44 shorter events, 5.1 us)
Async XLA Ops:
  0.6 66.5 %copy-start = (s32[96,5]{0,1:T(8,128)S(1)}, s32[96,5]{0,1:T(8,128)}, u32[]{:S(2)}) copy-start(s32[96,5]{0,1:T(8,128)} %param.9) | copy-start | bytes 5764
  2.6 15.4 %all-to-all-start = ((bf16[8,144,256]{2,1,0:T(8,128)(2,1)}), bf16[8,144,256]{2,1,0:T(8,128)(2,1)S(1)}, u32[]{:S(2)}, u32[]{:S(2)}) async-start(bf16[8,144,256]{2,1,0:T(8,128)(2,1)} %pack.6), calls=%async_computation | async-start | bytes 1179648 | tf_op jit(solution)/shard_map/all_to_all | solution.py:216
  18.0 14.5 %all-to-all-start.1 = ((bf16[8,144,256]{2,1,0:T(8,128)(2,1)}), bf16[8,144,256]{2,1,0:T(8,128)(2,1)S(1)}, u32[]{:S(2)}, u32[]{:S(2)}) async-start(bf16[8,144,256]{2,1,0:T(8,128)(2,1)} %pack.7), calls=%async_computation.1 | async-start | bytes 1179648 | tf_op jit(solution)/shard_map/all_to_all | solution.py:216
  32.5 14.5 %all-to-all-start.5 = ((bf16[8,144,256]{2,1,0:T(8,128)(2,1)}), bf16[8,144,256]{2,1,0:T(8,128)(2,1)S(1)}, u32[]{:S(2)}, u32[]{:S(2)}) async-start(bf16[8,144,256]{2,1,0:T(8,128)(2,1)} %pack.9), calls=%async_computation.5 | async-start | bytes 1179648 | tf_op jit(solution)/shard_map/all_to_all | solution.py:216
  47.0 15.4 %all-to-all-start.9 = ((bf16[8,144,256]{2,1,0:T(8,128)(2,1)}), bf16[8,144,256]{2,1,0:T(8,128)(2,1)S(1)}, u32[]{:S(2)}, u32[]{:S(2)}) async-start(bf16[8,144,256]{2,1,0:T(8,128)(2,1)} %pack.11), calls=%async_computation.9 | async-start | bytes 1179648 | tf_op jit(solution)/shard_map/all_to_all | solution.py:216
  50.6 33.4 %collective-permute-start = (bf16[1152,256]{1,0:T(8,128)(2,1)S(1)}, bf16[1152,256]{1,0:T(8,128)(2,1)S(1)}, u32[]{:S(2)}, u32[]{:S(2)}) collective-permute-start(bf16[1152,256]{1,0:T(8,128)(2,1)S(1)} %bitcast.19), channel_id=1, source_target_pairs={{0,8},{8,16},{16,24},{24,32},{32,40},{40,48},{48,56},{56,64},{64,7... | collective-permute-start | bytes 1769480 | tf_op jit(solution)/shard_map/ppermute | solution.py:223
  54.4 36.4 %collective-permute-start.1 = (bf16[1152,256]{1,0:T(8,128)(2,1)S(1)}, bf16[1152,256]{1,0:T(8,128)(2,1)}, u32[]{:S(2)}, u32[]{:S(2)}) collective-permute-start(bf16[1152,256]{1,0:T(8,128)(2,1)S(1)} %bitcast.20), channel_id=1, source_target_pairs={{8,0},{16,8},{24,16},{32,24},{40,32},{48,40},{56,48},{64,56},{72,6... | collective-permute-start | bytes 1769480 | tf_op jit(solution)/shard_map/ppermute | solution.py:224
  62.4 21.6 %copy-start.1 = (bf16[8,144,256]{2,1,0:T(8,128)(2,1)}, bf16[8,144,256]{2,1,0:T(8,128)(2,1)S(1)}, u32[]{:S(2)}) copy-start(bf16[8,144,256]{2,1,0:T(8,128)(2,1)S(1)} %all-to-all-done.9) | copy-start | bytes 1769476
  62.4 16.7 %all-to-all-start.4 = ((bf16[8,144,256]{2,1,0:T(8,128)(2,1)}), bf16[8,144,256]{2,1,0:T(8,128)(2,1)S(1)}, u32[]{:S(2)}, u32[]{:S(2)}) async-start(bf16[8,144,256]{2,1,0:T(8,128)(2,1)} %pack.8), calls=%async_computation.4 | async-start | bytes 1179648 | tf_op jit(solution)/shard_map/all_to_all | solution.py:216
  67.3 49.5 %collective-permute-start.4 = (bf16[1152,256]{1,0:T(8,128)(2,1)S(1)}, bf16[1152,256]{1,0:T(8,128)(2,1)}, u32[]{:S(2)}, u32[]{:S(2)}) collective-permute-start(bf16[1152,256]{1,0:T(8,128)(2,1)S(1)} %bitcast.15), channel_id=1, source_target_pairs={{0,8},{8,16},{16,24},{24,32},{32,40},{40,48},{48,56},{56,64},{64,7... | collective-permute-start | bytes 1769480 | tf_op jit(solution)/shard_map/ppermute | solution.py:223
  69.2 47.5 %collective-permute-start.5 = (bf16[1152,256]{1,0:T(8,128)(2,1)S(1)}, bf16[1152,256]{1,0:T(8,128)(2,1)}, u32[]{:S(2)}, u32[]{:S(2)}) collective-permute-start(bf16[1152,256]{1,0:T(8,128)(2,1)S(1)} %bitcast.16), channel_id=1, source_target_pairs={{8,0},{16,8},{24,16},{32,24},{40,32},{48,40},{56,48},{64,56},{72,6... | collective-permute-start | bytes 1769480 | tf_op jit(solution)/shard_map/ppermute | solution.py:224
  77.2 71.4 %collective-permute-start.8 = (bf16[1152,256]{1,0:T(8,128)(2,1)S(1)}, bf16[1152,256]{1,0:T(8,128)(2,1)}, u32[]{:S(2)}, u32[]{:S(2)}) collective-permute-start(bf16[1152,256]{1,0:T(8,128)(2,1)S(1)} %bitcast.12), channel_id=1, source_target_pairs={{0,8},{8,16},{16,24},{24,32},{32,40},{40,48},{48,56},{56,64},{64,7... | collective-permute-start | bytes 1769480 | tf_op jit(solution)/shard_map/ppermute | solution.py:223
  79.2 11.7 %copy-start.3 = (bf16[8,144,256]{2,1,0:T(8,128)(2,1)}, bf16[8,144,256]{2,1,0:T(8,128)(2,1)S(1)}, u32[]{:S(2)}) copy-start(bf16[8,144,256]{2,1,0:T(8,128)(2,1)S(1)} %all-to-all-done.4) | copy-start | bytes 1769476
  79.2 32.8 %all-to-all-start.8 = ((bf16[8,144,256]{2,1,0:T(8,128)(2,1)}), bf16[8,144,256]{2,1,0:T(8,128)(2,1)}, u32[]{:S(2)}, u32[]{:S(2)}) async-start(bf16[8,144,256]{2,1,0:T(8,128)(2,1)} %pack.10), calls=%async_computation.8 | async-start | bytes 1179648 | tf_op jit(solution)/shard_map/all_to_all | solution.py:216
  84.0 0.8 copy-start.8
  84.8 63.8 %collective-permute-start.9 = (bf16[1152,256]{1,0:T(8,128)(2,1)S(1)}, bf16[1152,256]{1,0:T(8,128)(2,1)}, u32[]{:S(2)}, u32[]{:S(2)}) collective-permute-start(bf16[1152,256]{1,0:T(8,128)(2,1)S(1)} %bitcast.13), channel_id=1, source_target_pairs={{8,0},{16,8},{24,16},{32,24},{40,32},{48,40},{56,48},{64,56},{72,6... | collective-permute-start | bytes 1769480 | tf_op jit(solution)/shard_map/ppermute | solution.py:224
  90.9 1.1 copy-start.9
  111.3 0.7 copy-start.7
  112.0 31.8 %all-to-all-start.2 = ((bf16[8,144,128]{2,1,0:T(8,128)(2,1)}), bf16[8,144,128]{2,1,0:T(8,128)(2,1)}, u32[]{:S(2)}, u32[]{:S(2)}) async-start(bf16[8,144,128]{2,1,0:T(8,128)(2,1)} %bitcast.25), calls=%async_computation.2 | async-start | bytes 589824 | tf_op jit(solution)/shard_map/all_to_all | solution.py:216
  116.8 1.1 copy-start.4
  137.2 0.7 copy-start.5
  137.9 43.8 %collective-permute-start.7 = (bf16[1152,256]{1,0:T(8,128)(2,1)}, bf16[1152,256]{1,0:T(8,128)(2,1)}, u32[]{:S(2)}, u32[]{:S(2)}) collective-permute-start(bf16[1152,256]{1,0:T(8,128)(2,1)} %get-tuple-element.28), channel_id=1, source_target_pairs={{8,0},{16,8},{24,16},{32,24},{40,32},{48,40},{56,48},{64,56},{72,6... | collective-permute-start | bytes 1769480 | tf_op jit(solution)/shard_map/ppermute | solution.py:224
  139.8 48.7 %collective-permute-start.6 = (bf16[1152,256]{1,0:T(8,128)(2,1)}, bf16[1152,256]{1,0:T(8,128)(2,1)}, u32[]{:S(2)}, u32[]{:S(2)}) collective-permute-start(bf16[1152,256]{1,0:T(8,128)(2,1)} %get-tuple-element.27), channel_id=1, source_target_pairs={{0,8},{8,16},{16,24},{24,32},{32,40},{40,48},{48,56},{56,64},{64,7... | collective-permute-start | bytes 1769480 | tf_op jit(solution)/shard_map/ppermute | solution.py:223
  143.8 39.9 %all-to-all-start.6 = ((bf16[8,144,128]{2,1,0:T(8,128)(2,1)}), bf16[8,144,128]{2,1,0:T(8,128)(2,1)}, u32[]{:S(2)}, u32[]{:S(2)}) async-start(bf16[8,144,128]{2,1,0:T(8,128)(2,1)} %bitcast.23), calls=%async_computation.6 | async-start | bytes 589824 | tf_op jit(solution)/shard_map/all_to_all | solution.py:216
  148.6 1.1 copy-start.2
  169.0 0.7 copy-start.6
  169.8 30.3 %collective-permute-start.11 = (bf16[1152,256]{1,0:T(8,128)(2,1)}, bf16[1152,256]{1,0:T(8,128)(2,1)}, u32[]{:S(2)}, u32[]{:S(2)}) collective-permute-start(bf16[1152,256]{1,0:T(8,128)(2,1)} %get-tuple-element.32), channel_id=1, source_target_pairs={{8,0},{16,8},{24,16},{32,24},{40,32},{48,40},{56,48},{64,56},{72,6... | collective-permute-start | bytes 1769480 | tf_op jit(solution)/shard_map/ppermute | solution.py:224
  173.8 26.3 %collective-permute-start.10 = (bf16[1152,256]{1,0:T(8,128)(2,1)}, bf16[1152,256]{1,0:T(8,128)(2,1)}, u32[]{:S(2)}, u32[]{:S(2)}) collective-permute-start(bf16[1152,256]{1,0:T(8,128)(2,1)} %get-tuple-element.31), channel_id=1, source_target_pairs={{0,8},{8,16},{16,24},{24,32},{32,40},{40,48},{48,56},{56,64},{64,7... | collective-permute-start | bytes 1769480 | tf_op jit(solution)/shard_map/ppermute | solution.py:223
  175.7 38.9 %collective-permute-start.3 = (bf16[1152,256]{1,0:T(8,128)(2,1)}, bf16[1152,256]{1,0:T(8,128)(2,1)}, u32[]{:S(2)}, u32[]{:S(2)}) collective-permute-start(bf16[1152,256]{1,0:T(8,128)(2,1)} %get-tuple-element.24), channel_id=1, source_target_pairs={{8,0},{16,8},{24,16},{32,24},{40,32},{48,40},{56,48},{64,56},{72,6... | collective-permute-start | bytes 1769480 | tf_op jit(solution)/shard_map/ppermute | solution.py:224
  181.8 32.8 %collective-permute-start.2 = (bf16[1152,256]{1,0:T(8,128)(2,1)}, bf16[1152,256]{1,0:T(8,128)(2,1)}, u32[]{:S(2)}, u32[]{:S(2)}) collective-permute-start(bf16[1152,256]{1,0:T(8,128)(2,1)} %get-tuple-element.23), channel_id=1, source_target_pairs={{0,8},{8,16},{16,24},{24,32},{32,40},{40,48},{48,56},{56,64},{64,7... | collective-permute-start | bytes 1769480 | tf_op jit(solution)/shard_map/ppermute | solution.py:223
  183.7 12.8 %all-to-all-start.10 = ((bf16[8,144,128]{2,1,0:T(8,128)(2,1)}), bf16[8,144,128]{2,1,0:T(8,128)(2,1)}, u32[]{:S(2)}, u32[]{:S(2)}) async-start(bf16[8,144,128]{2,1,0:T(8,128)(2,1)} %bitcast.24), calls=%async_computation.10 | async-start | bytes 589824 | tf_op jit(solution)/shard_map/all_to_all | solution.py:216
  196.5 14.5 %all-to-all-start.7 = ((bf16[8,144,256]{2,1,0:T(8,128)(2,1)}), bf16[8,144,256]{2,1,0:T(8,128)(2,1)S(1)}, u32[]{:S(2)}, u32[]{:S(2)}) async-start(bf16[8,144,256]{2,1,0:T(8,128)(2,1)} %bitcast.26), calls=%async_computation.7 | async-start | bytes 1179648 | tf_op jit(solution)/shard_map/all_to_all | solution.py:216
  211.0 5.9 %copy-start.10 = (bf16[8,144,256]{2,1,0:T(8,128)(2,1)}, bf16[8,144,256]{2,1,0:T(8,128)(2,1)S(1)}, u32[]{:S(2)}) copy-start(bf16[8,144,256]{2,1,0:T(8,128)(2,1)S(1)} %all-to-all-done.7.dkv_ref) | copy-start | bytes 1769476
  211.0 14.5 %all-to-all-start.11 = ((bf16[8,144,256]{2,1,0:T(8,128)(2,1)}), bf16[8,144,256]{2,1,0:T(8,128)(2,1)S(1)}, u32[]{:S(2)}, u32[]{:S(2)}) async-start(bf16[8,144,256]{2,1,0:T(8,128)(2,1)} %bitcast.11), calls=%async_computation.11 | async-start | bytes 1179648 | tf_op jit(solution)/shard_map/all_to_all | solution.py:216
  225.6 3.5 %copy-start.12 = (bf16[8,144,256]{2,1,0:T(8,128)(2,1)}, bf16[8,144,256]{2,1,0:T(8,128)(2,1)S(1)}, u32[]{:S(2)}) copy-start(bf16[8,144,256]{2,1,0:T(8,128)(2,1)S(1)} %all-to-all-done.11.dkv_ref) | copy-start | bytes 1769476
  225.6 14.5 %all-to-all-start.3 = ((bf16[8,144,256]{2,1,0:T(8,128)(2,1)}), bf16[8,144,256]{2,1,0:T(8,128)(2,1)S(1)}, u32[]{:S(2)}, u32[]{:S(2)}) async-start(bf16[8,144,256]{2,1,0:T(8,128)(2,1)} %bitcast.3), calls=%async_computation.3 | async-start | bytes 1179648 | tf_op jit(solution)/shard_map/all_to_all | solution.py:216
  240.1 0.8 copy-start.11
